TPU v7x, 32 devices: a whole 2x2x4 slice. The times are simulated.
32 devices in a mesh: grp: 2 (over y), row: 4 (over x, core), col: 4 (over z).
Axes of the slice: x: 2, y: 2, z: 4, core: 2. Of those that a mesh axis runs over, the one named last changes fastest.
Arguments:
- video: bfloat16 [514, 32, 512], P('grp', 'row', 'col'), parts along dimension 0, may hold values from -6 to 6, as said below
- filters: float32 [4, 2, 7, 7], replicated, may hold values from -0.875 to 0.875
- start_basis: float32 [256, 64], replicated, may hold values from -6 to 6
Outputs:
- basis: float32 [512, 64], P('grp'), parts along dimension 0
- modes: float32 [16, 128, 256], P(('grp', 'row'), 'col'), parts along dimension 0
There are 2 independent parts, one for each index of `grp`. A program takes and returns all parts, laid end to end along the dimension named above; an argument that names none is the same for every part. Nothing has to cross between parts.
Inputs may be any that keep to these rules, and one draw needn't show every extreme that they name: `video`: grey levels: a fixed texture plus a per-pixel oscillation in time.
All inputs are finite; a program needn't handle non-finite values.
Results may differ from a plain program's by a relative error of at most 0.0034.
Values may be sent and summed in bfloat16 or wider, within the bound.
No kernel may reach another device: no remote copies, remote signals or barrier semaphores. Data moves between devices by JAX's collectives and lax.ppermute only.
A program may use at most 64 MiB of HBM per device.

v0:
```python
import jax
import jax.numpy as jnp
from jax import lax
from jax.sharding import PartitionSpec as P

FRAMES = 256
MODES = 64
ORIENT = 4
TAPS = 7
SWEEPS = 2


def padded_2(array, sides, width):
    for axis, dim in sides:
        size, length = (lax.axis_size(axis), array.shape[dim])
        up = [(i, (i + 1) % size) for i in range(size - 1)]
        down = [(j, i) for i, j in up]
        last = lax.slice_in_dim(array, length - width, length, axis=dim)
        first = lax.slice_in_dim(array, 0, width, axis=dim)
        before = lax.ppermute(last, axis, up)
        after = lax.ppermute(first, axis, down)
        array = jnp.concatenate([before, array, after], axis=dim)
    return array


def orthonormal(stacked):
    inner = jnp.dot(stacked.T, stacked, precision=lax.Precision.HIGHEST)
    factor = jnp.linalg.cholesky(inner)
    return lax.linalg.triangular_solve(
        factor, stacked, left_side=False, lower=True, transpose_a=True
    )


def on_device(video, filters, start_basis):
    tile_rows = video.shape[1]
    tile_cols = video.shape[2]
    padded = padded_2(video, (("row", 1), ("col", 2)), 3)

    def orient(taps):
        kernels = taps.reshape(2, 1, TAPS, TAPS)
        lifted = padded.astype(jnp.float32)[:, None]
        response = lax.conv_general_dilated(
            lifted, kernels, (1, 1), "VALID", precision=lax.Precision.HIGHEST
        )
        real_part = response[:, 0]
        imag_part = response[:, 1]
        prod_real = real_part[1:] * real_part[:-1] + imag_part[1:] * imag_part[:-1]
        prod_imag = imag_part[1:] * real_part[:-1] - real_part[1:] * imag_part[:-1]
        motion = prod_imag / jnp.sqrt(prod_real * prod_real + prod_imag * prod_imag + 1.0)
        pooled = motion.reshape(FRAMES, tile_rows // 4, 4, tile_cols // 4, 4).mean(axis=(2, 4))
        return pooled.astype(jnp.bfloat16)

    stacked = lax.map(orient, filters)
    flat = jnp.transpose(stacked, (1, 0, 2, 3)).reshape(FRAMES, -1)
    devices_all = lax.axis_size("row") * lax.axis_size("col")
    npix_all = flat.shape[1] * devices_all
    basis_now = start_basis
    local_gram = jnp.dot(flat, flat.T, preferred_element_type=jnp.float32)
    gram = lax.psum(local_gram, ("row", "col")) / npix_all
    for sweep in range(SWEEPS):
        basis_now = orthonormal(jnp.dot(gram, basis_now, precision=lax.Precision.HIGHEST))
    projected = jnp.dot(basis_now.astype(jnp.bfloat16).T, flat, preferred_element_type=jnp.float32)
    fields = projected.reshape(MODES, ORIENT, tile_rows // 4, tile_cols // 4)
    modes = jnp.transpose(fields, (2, 3, 1, 0)).reshape(
        tile_rows // 4, tile_cols // 4, ORIENT * MODES
    )
    return (basis_now, modes)


def solution(mesh):
    return jax.shard_map(
        on_device,
        mesh=mesh,
        in_specs=(P("grp", "row", "col"), P(), P()),
        out_specs=(P("grp", None), P(("grp", "row"), "col", None)),
        check_vma=False,
    )
```

profile of v0, /device:TPU:1, one launch (start us, length us, event | category | flops | bytes accessed | tf_op | source)
XLA Modules:
  0.0 571.4 jit_solution(12141925055525839283)
XLA Ops:
  7.2 1.5 copy.25
  8.8 4.5 collective-permute-start
  13.3 1.9 collective-permute-start.1
  15.2 1.7 collective-permute-done
  16.9 4.4 collective-permute-done.1
  21.4 3.2 collective-permute-start.2
  24.6 1.3 collective-permute-start.3
  25.9 3.4 collective-permute-done.3
  29.3 1.8 pad_maximum_fusion
  31.1 414.1 %while.10 = (s32[]{:T(128)}, bf16[4,256,2,32]{1,3,2,0:T(8,128)(2,1)S(1)}, bf16[257,14,134]{0,2,1:T(8,128)(2,1)}, f32[4,2,7,7]{3,1,2,0:T(2,128)}, s32[]{:T(128)}) while((s32[]{:T(128)}, bf16[4,256,2,32]{1,3,2,0:T(8,128)(2,1)S(1)}, bf16[257,14,134]{0,2,1:T(8,128)(2,1)}, f32[4,2,7,7]{3,1,2,0:T(2,128)}, s32[]{:T(128)}) %tuple.29), condition=%wide.region_2.3_spmd, body=%wide.region_0.2_spmd.sunk | while | flops 312647680 | bytes 15818389 | solution.py:53
  31.1 0.7 dynamic-slice_bitcast_fusion.2
  32.0 87.6 %fusion.42 = f32[257,2,8,128]{0,1,3,2:T(2,128)S(1)} fusion(f32[2,1,7,7]{1,0,3,2:T(2,128)S(1)} %copy.40, bf16[257,1,14,134]{0,3,2,1:T(8,128)(2,1)} %bitcast.71), kind=kOutput, calls=%fused_computation.clone.1 | convolution fusion | flops 309485568 | bytes 3070000 | tf_op jit(solution)/shard_map/while/body/eval_jaxpr/conv_general_dilated | solution.py:42
  119.6 13.7 %multiply_reduce_fusion.4 = (f32[256,8,128]{0,2,1:T(8,128)S(1)}, f32[256,8,128]{0,2,1:T(8,128)S(1)}) fusion(f32[257,2,8,128]{0,1,3,2:T(2,128)S(1)} %fusion.42), kind=kLoop, calls=%fused_computation.3.clone.1 | loop fusion | flops 1835008 | bytes 6291456 | tf_op jit(solution)/shard_map/while/body/eval_jaxpr/mul | solution.py:49
  133.3 0.3 mul.70
  133.6 0.3 sub.13
  134.0 0.6 multiply_reduce_fusion.5
  134.6 0.7 dynamic-slice_bitcast_fusion.2
  135.5 87.6 %fusion.42 = f32[257,2,8,128]{0,1,3,2:T(2,128)S(1)} fusion(f32[2,1,7,7]{1,0,3,2:T(2,128)S(1)} %copy.40, bf16[257,1,14,134]{0,3,2,1:T(8,128)(2,1)} %bitcast.71), kind=kOutput, calls=%fused_computation.clone.1 | convolution fusion | flops 309485568 | bytes 3070000 | tf_op jit(solution)/shard_map/while/body/eval_jaxpr/conv_general_dilated | solution.py:42
  223.1 13.7 %multiply_reduce_fusion.4 = (f32[256,8,128]{0,2,1:T(8,128)S(1)}, f32[256,8,128]{0,2,1:T(8,128)S(1)}) fusion(f32[257,2,8,128]{0,1,3,2:T(2,128)S(1)} %fusion.42), kind=kLoop, calls=%fused_computation.3.clone.1 | loop fusion | flops 1835008 | bytes 6291456 | tf_op jit(solution)/shard_map/while/body/eval_jaxpr/mul | solution.py:49
  236.8 0.3 mul.70
  237.1 0.3 sub.13
  237.4 0.6 multiply_reduce_fusion.5
  238.1 0.7 dynamic-slice_bitcast_fusion.2
  239.0 87.6 %fusion.42 = f32[257,2,8,128]{0,1,3,2:T(2,128)S(1)} fusion(f32[2,1,7,7]{1,0,3,2:T(2,128)S(1)} %copy.40, bf16[257,1,14,134]{0,3,2,1:T(8,128)(2,1)} %bitcast.71), kind=kOutput, calls=%fused_computation.clone.1 | convolution fusion | flops 309485568 | bytes 3070000 | tf_op jit(solution)/shard_map/while/body/eval_jaxpr/conv_general_dilated | solution.py:42
  326.6 13.7 %multiply_reduce_fusion.4 = (f32[256,8,128]{0,2,1:T(8,128)S(1)}, f32[256,8,128]{0,2,1:T(8,128)S(1)}) fusion(f32[257,2,8,128]{0,1,3,2:T(2,128)S(1)} %fusion.42), kind=kLoop, calls=%fused_computation.3.clone.1 | loop fusion | flops 1835008 | bytes 6291456 | tf_op jit(solution)/shard_map/while/body/eval_jaxpr/mul | solution.py:49
  340.3 0.3 mul.70
  340.6 0.3 sub.13
  340.9 0.6 multiply_reduce_fusion.5
  341.6 0.7 dynamic-slice_bitcast_fusion.2
  342.5 87.6 %fusion.42 = f32[257,2,8,128]{0,1,3,2:T(2,128)S(1)} fusion(f32[2,1,7,7]{1,0,3,2:T(2,128)S(1)} %copy.40, bf16[257,1,14,134]{0,3,2,1:T(8,128)(2,1)} %bitcast.71), kind=kOutput, calls=%fused_computation.clone.1 | convolution fusion | flops 309485568 | bytes 3070000 | tf_op jit(solution)/shard_map/while/body/eval_jaxpr/conv_general_dilated | solution.py:42
  430.1 13.7 %multiply_reduce_fusion.4 = (f32[256,8,128]{0,2,1:T(8,128)S(1)}, f32[256,8,128]{0,2,1:T(8,128)S(1)}) fusion(f32[257,2,8,128]{0,1,3,2:T(2,128)S(1)} %fusion.42), kind=kLoop, calls=%fused_computation.3.clone.1 | loop fusion | flops 1835008 | bytes 6291456 | tf_op jit(solution)/shard_map/while/body/eval_jaxpr/mul | solution.py:49
  443.8 0.3 mul.70
  444.1 0.3 sub.13
  444.4 0.6 multiply_reduce_fusion.5
  445.2 0.9 convolution_bitcast_fusion
  446.2 89.3 %all-reduce.2.cloned.1.call-done = f32[256,256]{1,0:T(8,128)} async-done(((f32[256,256]{1,0:T(8,128)}), f32[256,256]{1,0:T(8,128)}) %all-reduce.2.cloned.1.call-update) | async-done | bytes 262160 | tf_op jit(solution)/shard_map/psum | solution.py:59
  535.5 1.3 fusion.6
  537.2 5.8 %cholesky.44 = f32[64,64]{1,0:T(8,128)S(1)} custom-call(f32[64,64]{1,0:T(8,128)S(1)} %fusion.18), custom_call_target="Cholesky" | custom-call | tf_op jit(solution)/shard_map/jit(cholesky)/cholesky | solution.py:28
  543.0 0.6 compare_reduce_fusion.1
  543.7 0.7 fusion.12
  544.3 4.9 custom-call.6
  549.2 0.3 convolution_bitcast_fusion.3
  549.5 1.3 fusion.4
  551.1 5.8 %cholesky.55 = f32[64,64]{1,0:T(8,128)S(1)} custom-call(f32[64,64]{1,0:T(8,128)S(1)} %fusion.16), custom_call_target="Cholesky" | custom-call | tf_op jit(solution)/shard_map/jit(cholesky)/cholesky | solution.py:28
  557.0 0.6 compare_reduce_fusion
  557.7 0.7 fusion.13
  558.3 4.9 custom-call.7
  563.8 0.8 reshape.57
  (29 shorter events, 2.1 us)
Async XLA Ops:
  7.2 528.4 %copy-start = (f32[256,64]{0,1:T(8,128)S(1)}, f32[256,64]{0,1:T(8,128)}, u32[]{:S(2)}) copy-start(f32[256,64]{0,1:T(8,128)} %param.10) | copy-start | bytes 196612
  7.2 528.3 %all-reduce.2.cloned.1.call-start = ((), (), s32[]{:S(2)}) async-start(), calls=%async_computation | async-start | bytes 524288 | tf_op jit(solution)/shard_map/psum | solution.py:59
  8.8 8.2 %collective-permute-start = (bf16[257,3,128]{0,2,1:T(8,128)(2,1)S(1)}, bf16[257,3,128]{0,2,1:T(8,128)(2,1)S(1)}, u32[]{:S(2)}, u32[]{:S(2)}) collective-permute-start(bf16[257,3,128]{0,2,1:T(8,128)(2,1)S(1)} %get-tuple-element.39), channel_id=1, source_target_pairs={{0,4},{4,8},{8,12},{1,5},{5,9},{9,13},{2,6},{6,10},{10,14},{3,7},{... | collective-permute-start | bytes 592136 | tf_op jit(solution)/shard_map/ppermute | solution.py:20
  13.3 8.0 %collective-permute-start.1 = (bf16[257,3,128]{0,2,1:T(8,128)(2,1)S(1)}, bf16[257,3,128]{0,2,1:T(8,128)(2,1)S(1)}, u32[]{:S(2)}, u32[]{:S(2)}) collective-permute-start(bf16[257,3,128]{0,2,1:T(8,128)(2,1)S(1)} %get-tuple-element.40), channel_id=1, source_target_pairs={{4,0},{8,4},{12,8},{5,1},{9,5},{13,9},{6,2},{10,6},{14,10},{7,3},{... | collective-permute-start | bytes 592136 | tf_op jit(solution)/shard_map/ppermute | solution.py:21
  21.4 4.5 collective-permute-start.2
  24.6 4.8 collective-permute-start.3
  563.5 1.0 copy-start.1
Sparse Core Ops, SparseCore 0:
  446.3 89.1 all-reduce.1
where the time goes:
time: 572 us; the launch traced here: 571 us
  matrix products  355 us (62%)
  waiting for transfers between devices  98.9 us (17%)
  other arithmetic  83.2 us (15%)
  between operations  14.2 us (2%)
  starting transfers between devices  11 us (2%)
  local copies, waits for them, and re-layouts  8.54 us (1%)
    conv_general_dilated x4, matrix products, orient(): lax.conv_general_dilated(lifted, kernels, (1, 1), 'VALID', precision=lax....  350 us
    psum x1, waiting for transfers between devices, on_device(): gram = lax.psum(local_gram, ('row', 'col')) / npix_all  89.3 us
    mul x4, other arithmetic, orient(): prod_real * prod_real + prod_imag * prod_imag + 1.0  54.8 us
    another operation x6, other arithmetic, orthonormal(): factor = jnp.linalg.cholesky(inner)  13 us
  transfers between devices with their start and end apart: 5, of which 4 were waited for; matrix products, arithmetic and copies ran while one was open for 0% of the time, Pallas kernels for 0%

commit v1 on v0

--- a/solution.py
+++ b/solution.py
@@ -56,7 +56,7 @@
     npix_all = flat.shape[1] * devices_all
     basis_now = start_basis
     local_gram = jnp.dot(flat, flat.T, preferred_element_type=jnp.float32)
-    gram = lax.psum(local_gram, ("row", "col")) / npix_all
+    gram = jnp.sum(lax.all_gather(local_gram, ("row", "col")), axis=0) / npix_all
     for sweep in range(SWEEPS):
         basis_now = orthonormal(jnp.dot(gram, basis_now, precision=lax.Precision.HIGHEST))
     projected = jnp.dot(basis_now.astype(jnp.bfloat16).T, flat, preferred_element_type=jnp.float32)

time: 572 us -> 534 us (0.934)
  waiting for transfers between devices: 98.9 us -> 60.4 us
    psum x1 -> x0, waiting for transfers between devices: 89.3 us -> none  [on_device(): gram = lax.psum(local_gram, ('row', 'col')) / npix_all]
    all_gather x0 -> x1, waiting for transfers between devices: none -> 50.9 us  [on_device(): lax.all_gather(local_gram, ('row', 'col'))]
where the time goes in v1:
time: 534 us
  matrix products  353 us (66%)
  other arithmetic  85.7 us (16%)
  waiting for transfers between devices  60.4 us (11%)
  between operations  14.2 us (3%)
  starting transfers between devices  11 us (2%)
  local copies, waits for them, and re-layouts  8.53 us (2%)
    conv_general_dilated x4, matrix products, orient(): lax.conv_general_dilated(lifted, kernels, (1, 1), 'VALID', precision=lax....  350 us
    mul x4, other arithmetic, orient(): prod_real * prod_real + prod_imag * prod_imag + 1.0  54.8 us
    all_gather x1, waiting for transfers between devices, on_device(): lax.all_gather(local_gram, ('row', 'col'))  50.9 us
    another operation x6, other arithmetic, orthonormal(): factor = jnp.linalg.cholesky(inner)  13 us
    another operation x4, other arithmetic, orthonormal(): lax.linalg.triangular_solve(factor, stacked, left_side=False, lower=True,...  11.1 us
  transfers between devices with their start and end apart: 5, of which 4 were waited for; matrix products, arithmetic and copies ran while one was open for 0% of the time, Pallas kernels for 0%

profile of v1, /device:TPU:1, one launch (start us, length us, event | category | flops | bytes accessed | tf_op | source)
XLA Modules:
  0.0 533.5 jit_solution(459961156083617008)
XLA Ops:
  7.2 1.5 copy.25
  8.8 4.5 collective-permute-start
  13.3 1.9 collective-permute-start.1
  15.2 1.7 collective-permute-done
  16.9 4.4 collective-permute-done.1
  21.4 3.2 collective-permute-start.2
  24.6 1.3 collective-permute-start.3
  25.9 3.4 collective-permute-done.3
  29.3 1.8 pad_maximum_fusion
  31.1 414.1 %while.10 = (s32[]{:T(128)}, bf16[4,256,2,32]{1,3,2,0:T(8,128)(2,1)S(1)}, bf16[257,14,134]{0,2,1:T(8,128)(2,1)}, f32[4,2,7,7]{3,1,2,0:T(2,128)}, s32[]{:T(128)}) while((s32[]{:T(128)}, bf16[4,256,2,32]{1,3,2,0:T(8,128)(2,1)S(1)}, bf16[257,14,134]{0,2,1:T(8,128)(2,1)}, f32[4,2,7,7]{3,1,2,0:T(2,128)}, s32[]{:T(128)}) %tuple.29), condition=%wide.region_2.3_spmd, body=%wide.region_0.2_spmd.sunk | while | flops 312647680 | bytes 15818389 | solution.py:53
  31.1 0.7 dynamic-slice_bitcast_fusion.2
  32.0 87.6 %fusion.42 = f32[257,2,8,128]{0,1,3,2:T(2,128)S(1)} fusion(f32[2,1,7,7]{1,0,3,2:T(2,128)S(1)} %copy.40, bf16[257,1,14,134]{0,3,2,1:T(8,128)(2,1)} %bitcast.72), kind=kOutput, calls=%fused_computation.clone.1 | convolution fusion | flops 309485568 | bytes 3070000 | tf_op jit(solution)/shard_map/while/body/eval_jaxpr/conv_general_dilated | solution.py:42
  119.6 13.7 %multiply_reduce_fusion.4 = (f32[256,8,128]{0,2,1:T(8,128)S(1)}, f32[256,8,128]{0,2,1:T(8,128)S(1)}) fusion(f32[257,2,8,128]{0,1,3,2:T(2,128)S(1)} %fusion.42), kind=kLoop, calls=%fused_computation.3.clone.1 | loop fusion | flops 1835008 | bytes 6291456 | tf_op jit(solution)/shard_map/while/body/eval_jaxpr/mul | solution.py:49
  133.3 0.3 mul.70
  133.6 0.3 sub.13
  134.0 0.6 multiply_reduce_fusion.5
  134.6 0.7 dynamic-slice_bitcast_fusion.2
  135.5 87.6 %fusion.42 = f32[257,2,8,128]{0,1,3,2:T(2,128)S(1)} fusion(f32[2,1,7,7]{1,0,3,2:T(2,128)S(1)} %copy.40, bf16[257,1,14,134]{0,3,2,1:T(8,128)(2,1)} %bitcast.72), kind=kOutput, calls=%fused_computation.clone.1 | convolution fusion | flops 309485568 | bytes 3070000 | tf_op jit(solution)/shard_map/while/body/eval_jaxpr/conv_general_dilated | solution.py:42
  223.1 13.7 %multiply_reduce_fusion.4 = (f32[256,8,128]{0,2,1:T(8,128)S(1)}, f32[256,8,128]{0,2,1:T(8,128)S(1)}) fusion(f32[257,2,8,128]{0,1,3,2:T(2,128)S(1)} %fusion.42), kind=kLoop, calls=%fused_computation.3.clone.1 | loop fusion | flops 1835008 | bytes 6291456 | tf_op jit(solution)/shard_map/while/body/eval_jaxpr/mul | solution.py:49
  236.8 0.3 mul.70
  237.1 0.3 sub.13
  237.4 0.6 multiply_reduce_fusion.5
  238.1 0.7 dynamic-slice_bitcast_fusion.2
  239.0 87.6 %fusion.42 = f32[257,2,8,128]{0,1,3,2:T(2,128)S(1)} fusion(f32[2,1,7,7]{1,0,3,2:T(2,128)S(1)} %copy.40, bf16[257,1,14,134]{0,3,2,1:T(8,128)(2,1)} %bitcast.72), kind=kOutput, calls=%fused_computation.clone.1 | convolution fusion | flops 309485568 | bytes 3070000 | tf_op jit(solution)/shard_map/while/body/eval_jaxpr/conv_general_dilated | solution.py:42
  326.6 13.7 %multiply_reduce_fusion.4 = (f32[256,8,128]{0,2,1:T(8,128)S(1)}, f32[256,8,128]{0,2,1:T(8,128)S(1)}) fusion(f32[257,2,8,128]{0,1,3,2:T(2,128)S(1)} %fusion.42), kind=kLoop, calls=%fused_computation.3.clone.1 | loop fusion | flops 1835008 | bytes 6291456 | tf_op jit(solution)/shard_map/while/body/eval_jaxpr/mul | solution.py:49
  340.3 0.3 mul.70
  340.6 0.3 sub.13
  340.9 0.6 multiply_reduce_fusion.5
  341.6 0.7 dynamic-slice_bitcast_fusion.2
  342.5 87.6 %fusion.42 = f32[257,2,8,128]{0,1,3,2:T(2,128)S(1)} fusion(f32[2,1,7,7]{1,0,3,2:T(2,128)S(1)} %copy.40, bf16[257,1,14,134]{0,3,2,1:T(8,128)(2,1)} %bitcast.72), kind=kOutput, calls=%fused_computation.clone.1 | convolution fusion | flops 309485568 | bytes 3070000 | tf_op jit(solution)/shard_map/while/body/eval_jaxpr/conv_general_dilated | solution.py:42
  430.1 13.7 %multiply_reduce_fusion.4 = (f32[256,8,128]{0,2,1:T(8,128)S(1)}, f32[256,8,128]{0,2,1:T(8,128)S(1)}) fusion(f32[257,2,8,128]{0,1,3,2:T(2,128)S(1)} %fusion.42), kind=kLoop, calls=%fused_computation.3.clone.1 | loop fusion | flops 1835008 | bytes 6291456 | tf_op jit(solution)/shard_map/while/body/eval_jaxpr/mul | solution.py:49
  443.8 0.3 mul.70
  444.1 0.3 sub.13
  444.4 0.6 multiply_reduce_fusion.5
  445.2 0.9 convolution_bitcast_fusion
  446.2 50.9 %all-gather.3.cloned.1.call-done = f32[4096,256]{1,0:T(8,128)} async-done(((f32[256,256]{1,0:T(8,128)}), f32[4096,256]{1,0:T(8,128)}) %all-gather.3.cloned.1.call-update) | async-done | bytes 4194320 | tf_op jit(solution)/shard_map/all_gather | solution.py:59
  497.0 2.5 reduce_sum.18
  499.5 0.4 fusion.6
  500.2 5.8 %cholesky.44 = f32[64,64]{1,0:T(8,128)S(1)} custom-call(f32[64,64]{1,0:T(8,128)S(1)} %fusion.18), custom_call_target="Cholesky" | custom-call | tf_op jit(solution)/shard_map/jit(cholesky)/cholesky | solution.py:28
  506.1 0.6 compare_reduce_fusion.1
  506.7 0.7 fusion.12
  507.4 4.9 custom-call.6
  512.6 0.4 fusion.4
  513.2 5.8 %cholesky.55 = f32[64,64]{1,0:T(8,128)S(1)} custom-call(f32[64,64]{1,0:T(8,128)S(1)} %fusion.16), custom_call_target="Cholesky" | custom-call | tf_op jit(solution)/shard_map/jit(cholesky)/cholesky | solution.py:28
  519.1 0.6 compare_reduce_fusion
  519.8 0.7 fusion.13
  520.4 4.9 custom-call.7
  525.9 0.8 reshape.57
  (30 shorter events, 2.4 us)
Async XLA Ops:
  7.2 492.4 %copy-start = (f32[256,64]{0,1:T(8,128)S(1)}, f32[256,64]{0,1:T(8,128)}, u32[]{:S(2)}) copy-start(f32[256,64]{0,1:T(8,128)} %param.10) | copy-start | bytes 196612
  7.2 489.9 %all-gather.3.cloned.1.call-start = ((), (), s32[]{:S(2)}) async-start(), calls=%async_computation | async-start | bytes 4456448 | tf_op jit(solution)/shard_map/all_gather | solution.py:59
  8.8 8.2 %collective-permute-start = (bf16[257,3,128]{0,2,1:T(8,128)(2,1)S(1)}, bf16[257,3,128]{0,2,1:T(8,128)(2,1)S(1)}, u32[]{:S(2)}, u32[]{:S(2)}) collective-permute-start(bf16[257,3,128]{0,2,1:T(8,128)(2,1)S(1)} %get-tuple-element.39), channel_id=1, source_target_pairs={{0,4},{4,8},{8,12},{1,5},{5,9},{9,13},{2,6},{6,10},{10,14},{3,7},{... | collective-permute-start | bytes 592136 | tf_op jit(solution)/shard_map/ppermute | solution.py:20
  13.3 8.0 %collective-permute-start.1 = (bf16[257,3,128]{0,2,1:T(8,128)(2,1)S(1)}, bf16[257,3,128]{0,2,1:T(8,128)(2,1)S(1)}, u32[]{:S(2)}, u32[]{:S(2)}) collective-permute-start(bf16[257,3,128]{0,2,1:T(8,128)(2,1)S(1)} %get-tuple-element.40), channel_id=1, source_target_pairs={{4,0},{8,4},{12,8},{5,1},{9,5},{13,9},{6,2},{10,6},{14,10},{7,3},{... | collective-permute-start | bytes 592136 | tf_op jit(solution)/shard_map/ppermute | solution.py:21
  21.4 4.5 collective-permute-start.2
  24.6 4.8 collective-permute-start.3
  525.6 1.0 copy-start.1
Sparse Core Ops, SparseCore 0:
  446.3 50.6 all-gather.2
